TPU v7x, 32 devices: a whole 2x2x4 slice. The times are simulated.
32 devices in a mesh: dp: 8 (over z, x), tensor: 4 (over y, core).
Axes of the slice: x: 2, y: 2, z: 4, core: 2. Of those that a mesh axis runs over, the one named last changes fastest.
Arguments:
- tokens: bfloat16 [8192, 1024], P('dp'), may hold values from -6 to 6
- segments: int32 [8192], P('dp'), may hold values from -1 to 26, as said below
- cotangent: bfloat16 [8192, 1024], P('dp'), may hold values from -6 to 6
- param_heads: float32 [3, 1024, 1024], P(None, 'dp', 'tensor'), may hold values from -0.1875 to 0.1875
- param_biases: float32 [2, 128, 8], P(None, 'tensor', 'dp'), may hold values from -1.5 to 1.5
- param_mixer: float32 [1024, 1024], P('tensor', 'dp'), may hold values from -1.5 to 1.5
- param_expand: float32 [1024, 4096], P('dp', 'tensor'), may hold values from -0.1875 to 0.1875
- param_offset: float32 [512, 8], P('tensor', 'dp'), may hold values from -2.5 to 2.5
- param_shrink: float32 [4096, 1024], P('tensor', 'dp'), may hold values from -0.09375 to 0.09375
- param_vector: float32 [8, 1024], P(None, 'dp'), may hold values from -0.8 to 1.6
- moment_heads: float32 [3, 1024, 1024], P(None, 'dp', 'tensor'), may hold values from -100 to 100
- moment_biases: float32 [2, 128, 8], P(None, 'tensor', 'dp'), may hold values from -100 to 100
- moment_mixer: float32 [1024, 1024], P('tensor', 'dp'), may hold values from -100 to 100
- moment_expand: float32 [1024, 4096], P('dp', 'tensor'), may hold values from -100 to 100
- moment_offset: float32 [512, 8], P('tensor', 'dp'), may hold values from -100 to 100
- moment_shrink: float32 [4096, 1024], P('tensor', 'dp'), may hold values from -100 to 100
- moment_vector: float32 [8, 1024], P(None, 'dp'), may hold values from -100 to 100
- square_heads: float32 [3, 1024, 1024], P(None, 'dp', 'tensor'), may hold values from 100 to 100000
- square_biases: float32 [2, 128, 8], P(None, 'tensor', 'dp'), may hold values from 100 to 100000
- square_mixer: float32 [1024, 1024], P('tensor', 'dp'), may hold values from 100 to 100000
- square_expand: float32 [1024, 4096], P('dp', 'tensor'), may hold values from 100 to 100000
- square_offset: float32 [512, 8], P('tensor', 'dp'), may hold values from 100 to 100000
- square_shrink: float32 [4096, 1024], P('tensor', 'dp'), may hold values from 100 to 100000
- square_vector: float32 [8, 1024], P(None, 'dp'), may hold values from 100 to 100000
Outputs:
- layer_output: bfloat16 [8192, 1024], P('dp')
- input_gradient: bfloat16 [8192, 1024], P('dp')
- direction_heads: float32 [3, 1024, 1024], P(None, 'dp', 'tensor')
- direction_biases: float32 [2, 128, 8], P(None, 'tensor', 'dp')
- direction_mixer: float32 [1024, 1024], P('tensor', 'dp')
- direction_expand: float32 [1024, 4096], P('dp', 'tensor')
- direction_offset: float32 [512, 8], P('tensor', 'dp')
- direction_shrink: float32 [4096, 1024], P('tensor', 'dp')
- direction_vector: float32 [8, 1024], P(None, 'dp')
- momentum_heads: float32 [3, 1024, 1024], P(None, 'dp', 'tensor')
- momentum_biases: float32 [2, 128, 8], P(None, 'tensor', 'dp')
- momentum_mixer: float32 [1024, 1024], P('tensor', 'dp')
- momentum_expand: float32 [1024, 4096], P('dp', 'tensor')
- momentum_offset: float32 [512, 8], P('tensor', 'dp')
- momentum_shrink: float32 [4096, 1024], P('tensor', 'dp')
- momentum_vector: float32 [8, 1024], P(None, 'dp')
Inputs may be any that keep to these rules, and one draw needn't show every extreme that they name: `segments`: in each packed row of 1024 tokens the tokens with one nonnegative number form one contiguous item of 197 or 37 tokens; numbers count up from 0 along the row, and the row ends with one or more padding tokens numbered -1.
All inputs are finite; a program needn't handle non-finite values.
Results may differ from a plain program's by a relative error of at most 0.017.
Values may be sent and summed in bfloat16 or wider, within the bound.
A program may use at most 128 MiB of HBM per device.

v0:
```python
import jax
import jax.numpy as jnp
from jax import lax
from jax.sharding import PartitionSpec as P

HEAD = 64
ROW = 1024


NORM_EPS = 1e-06
NEGATIVE = -1e30
INV_ROOT_TWO = 0.7071067811865476
INV_ROOT_TAU = 0.3989422804014327
BETA_ONE = 0.9
BETA_TWO = 0.999
ADAM_EPS = 1e-08
WEIGHT_DECAY = 0.05
CORRECT_ONE = 0.9999734386011124
CORRECT_TWO = 0.0952078528862904


def normalize(stream):
    center = stream - jnp.mean(stream, -1, keepdims=True)
    inverse = lax.rsqrt(jnp.mean(center * center, -1, keepdims=True) + NORM_EPS)
    return (center * inverse, inverse)


def norm_back(grad_normed, gain, unit, inverse):
    scaled = grad_normed * gain
    return inverse * (
        scaled
        - jnp.mean(scaled, -1, keepdims=True)
        - unit * jnp.mean(scaled * unit, -1, keepdims=True)
    )


def gelu_slope(pre_act):
    normal_cdf = 0.5 * (1.0 + lax.erf(pre_act * INV_ROOT_TWO))
    return normal_cdf + pre_act * jnp.exp(-0.5 * pre_act * pre_act) * INV_ROOT_TAU


def allowed_pairs(segments, query_start, row_start, block_size):
    seg_block = lax.dynamic_slice_in_dim(segments, query_start, block_size, 0)
    query_place = query_start - row_start + jnp.arange(block_size)
    key_place = jnp.arange(ROW)
    same_item = (seg_block[:, None] == segments[None, :]) & (seg_block[:, None] >= 0)
    return same_item | (query_place[:, None] == key_place[None, :])


def block_scores(queries, key_rows, segments, query_start, row_start, block_size, scaling):
    query_block = lax.dynamic_slice_in_dim(queries, query_start, block_size, 0)
    scores = (
        jnp.einsum("qhd,khd->hqk", query_block, key_rows, preferred_element_type=jnp.float32)
        * scaling
    )
    allowed = allowed_pairs(segments, query_start, row_start, block_size)
    return (jnp.where(allowed[None], scores, NEGATIVE), query_block, key_rows)


def attend_forward(queries, key_rows, value_rows, segments, block_size):
    block_count = queries.shape[0] // block_size
    scaling = queries.shape[2] ** (-0.5)

    def forward_block(block_index):
        query_start = block_index * block_size
        row_start = query_start // ROW * ROW
        scores, query_block, key_block = block_scores(
            queries, key_rows, segments, query_start, row_start, block_size, scaling
        )
        highest = jnp.max(scores, -1, keepdims=True)
        expo = jnp.exp(scores - highest)
        total = jnp.sum(expo, -1, keepdims=True)
        chances = (expo / total).astype(jnp.bfloat16)
        mixed = jnp.einsum("hqk,khd->qhd", chances, value_rows, preferred_element_type=jnp.float32)
        return (mixed.astype(jnp.bfloat16), (highest + jnp.log(total))[..., 0])

    mixed_blocks, log_totals = lax.map(forward_block, jnp.arange(block_count))
    return (mixed_blocks.reshape(queries.shape[0], -1), log_totals)


def attend_backward(queries, key_rows, value_rows, segments, log_totals, grad_mixed, block_size):
    block_count = queries.shape[0] // block_size
    scaling = queries.shape[2] ** (-0.5)
    zero_grad = jnp.zeros(queries.shape, jnp.float32)

    def backward_block(totals, block_index):
        grad_query, grad_key, grad_value = totals
        query_start = block_index * block_size
        row_start = query_start // ROW * ROW
        scores, query_block, key_block = block_scores(
            queries, key_rows, segments, query_start, row_start, block_size, scaling
        )
        grad_block = lax.dynamic_slice_in_dim(grad_mixed, query_start, block_size, 0)
        chances = jnp.exp(scores - log_totals[block_index][..., None])
        grad_chance = jnp.einsum(
            "qhd,khd->hqk", grad_block, value_rows, preferred_element_type=jnp.float32
        )
        row_delta = jnp.sum(chances * grad_chance, -1, keepdims=True)
        grad_scores = (chances * (grad_chance - row_delta)).astype(jnp.bfloat16)
        part_query = (
            jnp.einsum("hqk,khd->qhd", grad_scores, key_block, preferred_element_type=jnp.float32)
            * scaling
        )
        part_key = (
            jnp.einsum("hqk,qhd->khd", grad_scores, query_block, preferred_element_type=jnp.float32)
            * scaling
        )
        part_value = jnp.einsum(
            "hqk,qhd->khd",
            chances.astype(jnp.bfloat16),
            grad_block,
            preferred_element_type=jnp.float32,
        )
        grad_query = lax.dynamic_update_slice_in_dim(grad_query, part_query, query_start, 0)
        grad_key = grad_key + part_key
        grad_value = grad_value + part_value
        return ((grad_query, grad_key, grad_value), None)

    results, _ = lax.scan(
        backward_block, (zero_grad, zero_grad, zero_grad), jnp.arange(block_count)
    )
    return results


def adamw(master, gradient, moment, square, decay_rate):
    moment = BETA_ONE * moment + (1.0 - BETA_ONE) * gradient
    square = BETA_TWO * square + (1.0 - BETA_TWO) * gradient * gradient
    change = moment / CORRECT_ONE / (jnp.sqrt(square / CORRECT_TWO) + ADAM_EPS)
    return (change + decay_rate * master, moment)


def shards(
    tokens,
    segments,
    cotangent,
    param_heads,
    param_biases,
    param_mixer,
    param_expand,
    param_offset,
    param_shrink,
    param_vector,
    moment_heads,
    moment_biases,
    moment_mixer,
    moment_expand,
    moment_offset,
    moment_shrink,
    moment_vector,
    square_heads,
    square_biases,
    square_mixer,
    square_expand,
    square_offset,
    square_shrink,
    square_vector,
):
    narrow = jnp.bfloat16
    wide = jnp.float32
    heads_w, biases_w, mixer_w, expand_w, offset_w, shrink_w, vector_w = (
        lax.all_gather(param_heads.astype(narrow), "dp", axis=1, tiled=True),
        lax.all_gather(param_biases.astype(narrow), "dp", axis=2, tiled=True),
        lax.all_gather(param_mixer.astype(narrow), "dp", axis=1, tiled=True),
        lax.all_gather(param_expand.astype(narrow), "dp", axis=0, tiled=True),
        lax.all_gather(param_offset.astype(narrow), "dp", axis=1, tiled=True),
        lax.all_gather(param_shrink.astype(narrow), "dp", axis=1, tiled=True),
        lax.all_gather(param_vector.astype(narrow), "dp", axis=1, tiled=True),
    )
    biases = biases_w.reshape(2, -1).astype(wide)
    offset = offset_w.reshape(-1).astype(wide)
    vectors = vector_w.astype(wide)
    token_count = tokens.shape[0]
    block_size = min(512, ROW)
    local_heads = heads_w.shape[2] // HEAD
    shaped = (token_count, local_heads, HEAD)
    stream = tokens.astype(wide)
    unit_one, inverse_one = normalize(stream)
    normed_one = (unit_one * vectors[0] + vectors[1]).astype(narrow)
    queries = (jnp.dot(normed_one, heads_w[0], preferred_element_type=wide) + biases[0]).astype(
        narrow
    )
    key_rows = jnp.dot(normed_one, heads_w[1], preferred_element_type=wide).astype(narrow)
    value_rows = (jnp.dot(normed_one, heads_w[2], preferred_element_type=wide) + biases[1]).astype(
        narrow
    )
    mixed_heads, log_totals = attend_forward(
        queries.reshape(shaped),
        key_rows.reshape(shaped),
        value_rows.reshape(shaped),
        segments,
        block_size,
    )
    attn_out = (
        lax.psum(
            jnp.dot(mixed_heads, mixer_w, preferred_element_type=wide).astype(jnp.bfloat16),
            "tensor",
        ).astype(jnp.float32)
        + vectors[2]
    )
    middle = stream + vectors[3] * attn_out
    unit_two, inverse_two = normalize(middle)
    normed_two = (unit_two * vectors[4] + vectors[5]).astype(narrow)
    pre_act = jnp.dot(normed_two, expand_w, preferred_element_type=wide) + offset
    activation = jax.nn.gelu(pre_act, approximate=False).astype(narrow)
    mlp_out = (
        lax.psum(
            jnp.dot(activation, shrink_w, preferred_element_type=wide).astype(jnp.bfloat16),
            "tensor",
        ).astype(jnp.float32)
        + vectors[6]
    )
    layer_output = (middle + vectors[7] * mlp_out).astype(narrow)
    grad_out = cotangent.astype(wide)
    grad_scale_two = jnp.sum(grad_out * mlp_out, 0)
    grad_mlp = (vectors[7] * grad_out).astype(narrow)
    grad_bias_out = jnp.sum(grad_mlp.astype(wide), 0)
    grad_shrink = jnp.einsum("tf,td->fd", activation, grad_mlp, preferred_element_type=wide)
    grad_act = jnp.einsum("td,fd->tf", grad_mlp, shrink_w, preferred_element_type=wide)
    grad_pre = (grad_act * gelu_slope(pre_act)).astype(narrow)
    grad_offset = jnp.sum(grad_pre.astype(wide), 0).reshape(offset_w.shape)
    grad_expand = jnp.einsum("tc,tf->cf", normed_two, grad_pre, preferred_element_type=wide)
    partial_two = jnp.einsum("tf,cf->tc", grad_pre, expand_w, preferred_element_type=wide)
    grad_normed_two = lax.psum(partial_two.astype(jnp.bfloat16), "tensor").astype(jnp.float32)
    grad_gain_two = jnp.sum(grad_normed_two * unit_two, 0)
    grad_shift_two = jnp.sum(grad_normed_two, 0)
    grad_middle = grad_out + norm_back(grad_normed_two, vectors[4], unit_two, inverse_two)
    grad_scale_one = jnp.sum(grad_middle * attn_out, 0)
    grad_attn = (vectors[3] * grad_middle).astype(narrow)
    grad_bias_mix = jnp.sum(grad_attn.astype(wide), 0)
    grad_mixer = jnp.einsum("tc,td->cd", mixed_heads, grad_attn, preferred_element_type=wide)
    grad_mixed = jnp.einsum("td,cd->tc", grad_attn, mixer_w, preferred_element_type=wide).astype(
        narrow
    )
    grad_query, grad_key, grad_value = attend_backward(
        queries.reshape(shaped),
        key_rows.reshape(shaped),
        value_rows.reshape(shaped),
        segments,
        log_totals,
        grad_mixed.reshape(shaped),
        block_size,
    )
    grad_triple = (
        jnp.stack([grad_query, grad_key, grad_value]).reshape(3, token_count, -1).astype(narrow)
    )
    grad_biases = jnp.stack(
        [jnp.sum(grad_triple[0].astype(wide), 0), jnp.sum(grad_triple[2].astype(wide), 0)]
    ).reshape(biases_w.shape)
    grad_heads = jnp.einsum("tc,jth->jch", normed_one, grad_triple, preferred_element_type=wide)
    partial_one = jnp.einsum("jth,jch->tc", grad_triple, heads_w, preferred_element_type=wide)
    grad_normed_one = lax.psum(partial_one.astype(jnp.bfloat16), "tensor").astype(jnp.float32)
    grad_gain_one = jnp.sum(grad_normed_one * unit_one, 0)
    grad_shift_one = jnp.sum(grad_normed_one, 0)
    grad_stream = grad_middle + norm_back(grad_normed_one, vectors[0], unit_one, inverse_one)
    input_gradient = grad_stream.astype(narrow)
    grad_vector = jnp.stack(
        [
            grad_gain_one,
            grad_shift_one,
            grad_bias_mix,
            grad_scale_one,
            grad_gain_two,
            grad_shift_two,
            grad_bias_out,
            grad_scale_two,
        ]
    )
    sum_heads, sum_biases, sum_mixer, sum_expand, sum_offset, sum_shrink, sum_vector = (
        lax.psum_scatter(grad_heads, "dp", scatter_dimension=1, tiled=True),
        lax.psum_scatter(grad_biases, "dp", scatter_dimension=2, tiled=True),
        lax.psum_scatter(grad_mixer, "dp", scatter_dimension=1, tiled=True),
        lax.psum_scatter(grad_expand, "dp", scatter_dimension=0, tiled=True),
        lax.psum_scatter(grad_offset, "dp", scatter_dimension=1, tiled=True),
        lax.psum_scatter(grad_shrink, "dp", scatter_dimension=1, tiled=True),
        lax.psum_scatter(grad_vector, "dp", scatter_dimension=1, tiled=True),
    )
    new_heads = adamw(param_heads, sum_heads, moment_heads, square_heads, WEIGHT_DECAY)
    new_biases = adamw(param_biases, sum_biases, moment_biases, square_biases, 0.0)
    new_mixer = adamw(param_mixer, sum_mixer, moment_mixer, square_mixer, WEIGHT_DECAY)
    new_expand = adamw(param_expand, sum_expand, moment_expand, square_expand, WEIGHT_DECAY)
    new_offset = adamw(param_offset, sum_offset, moment_offset, square_offset, 0.0)
    new_shrink = adamw(param_shrink, sum_shrink, moment_shrink, square_shrink, WEIGHT_DECAY)
    new_vector = adamw(param_vector, sum_vector, moment_vector, square_vector, 0.0)
    return (
        layer_output,
        input_gradient,
        new_heads[0],
        new_biases[0],
        new_mixer[0],
        new_expand[0],
        new_offset[0],
        new_shrink[0],
        new_vector[0],
        new_heads[1],
        new_biases[1],
        new_mixer[1],
        new_expand[1],
        new_offset[1],
        new_shrink[1],
        new_vector[1],
    )


def solution(mesh):
    in_specs = (
        P("dp", None),
        P("dp"),
        P("dp", None),
        P(None, "dp", "tensor"),
        P(None, "tensor", "dp"),
        P("tensor", "dp"),
        P("dp", "tensor"),
        P("tensor", "dp"),
        P("tensor", "dp"),
        P(None, "dp"),
        P(None, "dp", "tensor"),
        P(None, "tensor", "dp"),
        P("tensor", "dp"),
        P("dp", "tensor"),
        P("tensor", "dp"),
        P("tensor", "dp"),
        P(None, "dp"),
        P(None, "dp", "tensor"),
        P(None, "tensor", "dp"),
        P("tensor", "dp"),
        P("dp", "tensor"),
        P("tensor", "dp"),
        P("tensor", "dp"),
        P(None, "dp"),
    )
    out_specs = (
        P("dp", None),
        P("dp", None),
        P(None, "dp", "tensor"),
        P(None, "tensor", "dp"),
        P("tensor", "dp"),
        P("dp", "tensor"),
        P("tensor", "dp"),
        P("tensor", "dp"),
        P(None, "dp"),
        P(None, "dp", "tensor"),
        P(None, "tensor", "dp"),
        P("tensor", "dp"),
        P("dp", "tensor"),
        P("tensor", "dp"),
        P("tensor", "dp"),
        P(None, "dp"),
    )
    return jax.shard_map(shards, mesh=mesh, in_specs=in_specs, out_specs=out_specs, check_vma=False)
```

profile of v0, /device:TPU:0, one launch (start us, length us, event | category | flops | bytes accessed | tf_op | source)
XLA Modules:
  0.0 896.9 jit_solution(12945277225385575034)
XLA Ops:
  10.5 22.1 %all_gather.23 = bf16[2,32,8]{1,0,2:T(2,128)(2,1)S(1)} all-gather(bf16[2,32,1]{1,0,2:T(2,128)(2,1)S(1)} %convert_element_type.154), channel_id=1, replica_groups=mesh['dp'=8,'tensor'=4] {'dp'}, dimensions={2}, use_global_device_ids=true | all-gather | bytes 1152 | tf_op jit(solution)/shard_map/all_gather | solution.py:162
  33.9 26.1 %all_gather.21 = bf16[8,1024]{1,0:T(8,128)(2,1)S(1)} all-gather(bf16[8,128]{1,0:T(8,128)(2,1)S(1)} %convert_element_type.150), channel_id=1, replica_groups=mesh['dp'=8,'tensor'=4] {'dp'}, dimensions={1}, use_global_device_ids=true | all-gather | bytes 18432 | tf_op jit(solution)/shard_map/all_gather | solution.py:167
  63.4 28.1 %all_gather.24 = bf16[256,1024]{1,0:T(8,128)(2,1)} all-gather(bf16[256,128]{1,0:T(8,128)(2,1)S(1)} %convert_element_type.159), channel_id=1, replica_groups=mesh['dp'=8,'tensor'=4] {'dp'}, dimensions={1}, use_global_device_ids=true | all-gather | bytes 589824 | tf_op jit(solution)/shard_map/all_gather | solution.py:163
  101.4 19.8 %while.31 = (s32[]{:T(128)}, bf16[2,512,4,64]{1,3,2,0:T(8,128)(2,1)}, f32[2,4,512]{2,1,0:T(4,128)S(1)}, s32[2]{0:T(128)S(1)}, s32[1024]{0:T(1024)S(1)}, /*index=...) while((s32[]{:T(128)}, ...), condition=%wide.region_5.6_spmd, body=%wide.region_2.5_spmd.sunk | while | flops 564263936 | bytes 35208668 | solution.py:77
  128.7 16.6 %all-gather = bf16[8,1,128]{2,1,0:T(2,128)(2,1)S(1)} all-gather(bf16[1,1,128]{2,1,0:T(2,128)(2,1)S(1)} %convert_bitcast_fusion), channel_id=1, replica_groups=mesh['dp'=8,'tensor'=4] {'dp'}, dimensions={0}, use_global_device_ids=true | all-gather | bytes 2304 | tf_op jit(solution)/shard_map/all_gather | solution.py:165
  145.5 30.7 %all-reduce.8.cloned.1.call-done = bf16[1024,1024]{1,0:T(8,128)(2,1)} async-done(((bf16[1024,1024]{1,0:T(8,128)(2,1)}), bf16[1024,1024]{1,0:T(8,128)(2,1)}) %all-reduce.8.cloned.1.call-update) | async-done | bytes 2097168 | tf_op jit(solution)/shard_map/psum | solution.py:194
  182.7 45.8 %all-gather.7.cloned.1.call-done = bf16[1024,1024]{1,0:T(8,128)(2,1)} async-done(((bf16[128,1024]{1,0:T(8,128)(2,1)}), bf16[1024,1024]{1,0:T(8,128)(2,1)}) %all-gather.7.cloned.1.call-update) | async-done | bytes 2097168 | tf_op jit(solution)/shard_map/all_gather | solution.py:164
  228.5 14.3 %fusion.62 = (bf16[1024,1024]{1,0:T(8,128)(2,1)S(1)}, f32[1024,1024]{1,0:T(8,128)}) fusion(f32[1024]{0:T(1024)S(1)} %reshape.293, bf16[1024,1024]{1,0:T(8,128)(2,1)} %add_convert_fusion.1, bf16[1024,1024]{1,0:T(8,128)(2,1)} %all-gather.7.cloned.1.call-done), kind=kOutput, calls=%fused_computation.87 | convolution fusion | flops 2216689664 | bytes 10489856 | tf_op jit(solution)/shard_map/dot_general | solution.py:203
  248.6 86.9 %reduce-scatter.13.cloned.1.call-done = f32[1024,128]{1,0:T(8,128)} async-done(((f32[1024,1024]{1,0:T(8,128)}), f32[1024,128]{1,0:T(8,128)}) %reduce-scatter.13.cloned.1.call-update) | async-done | bytes 524304 | tf_op jit(solution)/shard_map/reduce_scatter | solution.py:274
  338.9 50.7 %all-gather.9.cloned.1.call-done = bf16[1024,1024]{1,0:T(8,128)(2,1)} async-done(((bf16[1024,128]{1,0:T(8,128)(2,1)}), bf16[1024,1024]{1,0:T(8,128)(2,1)}) %all-gather.9.cloned.1.call-update) | async-done | bytes 2097168 | tf_op jit(solution)/shard_map/all_gather | solution.py:166
  389.7 7.4 convert_reduce_fusion.5
  402.2 5.9 convolution_convert_fusion.1
  408.1 43.8 %all-reduce.10.cloned.1.call-done = bf16[1024,1024]{1,0:T(8,128)(2,1)} async-done(((bf16[1024,1024]{1,0:T(8,128)(2,1)}), bf16[1024,1024]{1,0:T(8,128)(2,1)}) %all-reduce.10.cloned.1.call-update) | async-done | bytes 2097168 | tf_op jit(solution)/shard_map/psum | solution.py:223
  451.9 4.8 fusion.71
  463.4 34.0 %while.32 = (s32[]{:T(128)}, bf16[1024,4,64]{0,2,1:T(8,128)(2,1)}, f32[1024,4,64]{0,2,1:T(8,128)}, f32[1024,4,64]{0,2,1:T(8,128)}, s32[2]{0:T(128)S(1)}, /*index...) while((s32[]{:T(128)}, bf16[1024,4,64]{0,2,1:T(8,128)(2,1)}, ...), condition=%wide.region_15.16_spmd.clone, body=%wide.region_13.15_spmd.clone.sunk | while | flops 1377172480 | bytes 97590984 | solution.py:119
  503.2 4.9 bitcast_convert_fusion
  512.5 81.6 %all-reduce.12.cloned.1.call-done = (bf16[1024,1024]{1,0:T(8,128)(2,1)}, bf16[1024,1024]{1,0:T(8,128)(2,1)}) async-done(((bf16[1024,1024]{1,0:T(8,128)(2,1)}, bf16[1024,1024]{1,0:T(8,128)(2,1)}), (bf16[1024,1024]{1,0:T(8,128)(2,1)}, bf16[1024,1024]{1,0:T(8,128)(2,1)})) %all-reduce.12.cloned.1.call-update) | async-done | bytes 4194320 | tf_op jit(solution)/shard_map/psum | solution.py:206
  597.8 7.5 fusion.64
  606.1 5.4 fusion.82
  611.6 5.9 fusion.130
  620.2 38.0 %all-reduce.2 = (f32[2,32,8]{1,0,2:T(2,128)S(1)}, f32[128,8]{1,0:T(8,128)S(1)}) all-reduce(f32[2,32,8]{1,0,2:T(2,128)S(1)} %copy.157, f32[128,8]{1,0:T(8,128)S(1)} %reshape.292), channel_id=3, replica_groups=mesh['dp'=8,'tensor'=4] {'dp'}, use_global_device_ids=true, to_apply=%region_22.23.clone | all-reduce | flops 1536 | bytes 12288
  664.0 54.3 %reduce-scatter.15.cloned.1.call-done = f32[8,128]{1,0:T(8,128)} async-done(((f32[8,1024]{1,0:T(8,128)}), f32[8,128]{1,0:T(8,128)}) %reduce-scatter.15.cloned.1.call-update) | async-done | bytes 4112 | tf_op jit(solution)/shard_map/reduce_scatter | solution.py:275
  719.6 76.6 %reduce-scatter.7.cloned.1.call-done = f32[3,128,256]{1,2,0:T(8,128)} async-done(((f32[3,1024,256]{1,2,0:T(8,128)}), f32[3,128,256]{1,2,0:T(8,128)}) %reduce-scatter.7.cloned.1.call-update) | async-done | bytes 393232 | tf_op jit(solution)/shard_map/reduce_scatter | solution.py:269
  799.3 88.0 %reduce-scatter.11.cloned.1.call-done = f32[128,1024]{1,0:T(8,128)} async-done(((f32[1024,1024]{1,0:T(8,128)}), f32[128,1024]{1,0:T(8,128)}) %reduce-scatter.11.cloned.1.call-update) | async-done | bytes 524304 | tf_op jit(solution)/shard_map/reduce_scatter | solution.py:272
  (263 shorter events, 129.0 us)
Async XLA Ops:
  7.2 54.8 %copy-start = (bf16[1024,1024]{1,0:T(8,128)(2,1)S(1)}, bf16[1024,1024]{1,0:T(8,128)(2,1)}, u32[]{:S(2)}) copy-start(bf16[1024,1024]{1,0:T(8,128)(2,1)} %param.28) | copy-start | bytes 6291460
  7.2 86.5 %all-gather.5.cloned.1.call-start = ((), (), s32[]{:S(2)}) async-start(), calls=%async_computation.5 | async-start | bytes 1769472 | tf_op jit(solution)/shard_map/all_gather | solution.py:161
  9.1 167.1 %all-reduce.8.cloned.1.call-start = ((), (), s32[]{:S(2)}) async-start(), calls=%async_computation.6 | async-start | bytes 4194304 | tf_op jit(solution)/shard_map/psum | solution.py:194
  62.0 31.6 %copy-start.36 = (f32[1024]{0:T(1024)}, f32[1024]{0:T(1024)S(1)}, u32[]{:S(2)}) copy-start(f32[1024]{0:T(1024)S(1)} %broadcast_multiply_fusion.5) | copy-start | bytes 12292
  126.8 101.7 %all-gather.7.cloned.1.call-start = ((), (), s32[]{:S(2)}) async-start(), calls=%async_computation.7 | async-start | bytes 2359296 | tf_op jit(solution)/shard_map/all_gather | solution.py:164
  128.6 207.0 %reduce-scatter.13.cloned.1.call-start = ((), (), s32[]{:S(2)}) async-start(), calls=%async_computation.13 | async-start | bytes 4718592 | tf_op jit(solution)/shard_map/reduce_scatter | solution.py:274
  248.6 141.1 %all-gather.9.cloned.1.call-start = ((), (), s32[]{:S(2)}) async-start(), calls=%async_computation.8 | async-start | bytes 2359296 | tf_op jit(solution)/shard_map/all_gather | solution.py:166
  338.7 113.2 %all-reduce.10.cloned.1.call-start = ((), (), s32[]{:S(2)}) async-start(), calls=%async_computation.9 | async-start | bytes 4194304 | tf_op jit(solution)/shard_map/psum | solution.py:223
  402.2 191.9 %all-reduce.12.cloned.1.call-start = ((), (), s32[]{:S(2)}) async-start(), calls=%async_computation.15 | async-start | bytes 8388608 | tf_op jit(solution)/shard_map/psum | solution.py:206
  508.1 85.9 %copy-start.37 = (f32[1024]{0:T(1024)S(1)}, f32[1024]{0:T(1024)}, u32[]{:S(2)}) copy-start(f32[1024]{0:T(1024)} %copy-done.36) | copy-start | bytes 12292
  508.1 85.9 %copy-start.39 = (f32[1,1024]{1,0:T(1,128)S(1)}, f32[1,1024]{1,0:T(1,128)}, u32[]{:S(2)}) copy-start(f32[1,1024]{1,0:T(1,128)} %copy-done.38) | copy-start | bytes 12292
  508.1 85.9 %copy-start.41 = (f32[1024]{0:T(1024)S(1)}, f32[1024]{0:T(1024)}, u32[]{:S(2)}) copy-start(f32[1024]{0:T(1024)} %copy-done.40) | copy-start | bytes 12292
  508.2 89.6 %copy-start.42 = (f32[1,1024]{1,0:T(1,128)S(1)}, f32[1,1024]{1,0:T(1,128)}, u32[]{:S(2)}) copy-start(f32[1,1024]{1,0:T(1,128)} %get-tuple-element.463) | copy-start | bytes 12292
  508.2 154.0 %reduce-scatter.9.cloned.1.call-start = ((), (), s32[]{:S(2)}) async-start(), calls=%async_computation.11 | async-start | bytes 1179648 | tf_op jit(solution)/shard_map/reduce_scatter | solution.py:271
  512.5 205.8 %reduce-scatter.15.cloned.1.call-start = ((), (), s32[]{:S(2)}) async-start(), calls=%async_computation.14 | async-start | bytes 36864 | tf_op jit(solution)/shard_map/reduce_scatter | solution.py:275
  606.0 190.2 %reduce-scatter.7.cloned.1.call-start = ((), (), s32[]{:S(2)}) async-start(), calls=%async_computation.10 | async-start | bytes 3538944 | tf_op jit(solution)/shard_map/reduce_scatter | solution.py:269
  611.5 275.8 %reduce-scatter.11.cloned.1.call-start = ((), (), s32[]{:S(2)}) async-start(), calls=%async_computation.12 | async-start | bytes 4718592 | tf_op jit(solution)/shard_map/reduce_scatter | solution.py:272
  617.6 44.6 %copy-start.31 = (f32[256,128]{1,0:T(8,128)S(1)}, f32[256,128]{1,0:T(8,128)}, u32[]{:S(2)}) copy-start(f32[256,128]{1,0:T(8,128)} %param.33) | copy-start | bytes 393220
  617.6 44.6 %copy-start.35 = (f32[256,128]{1,0:T(8,128)S(1)}, f32[256,128]{1,0:T(8,128)}, u32[]{:S(2)}) copy-start(f32[256,128]{1,0:T(8,128)} %param.47) | copy-start | bytes 393220
  617.6 100.7 %copy-start.43 = (f32[8,128]{1,0:T(8,128)S(1)}, f32[8,128]{1,0:T(8,128)}, u32[]{:S(2)}) copy-start(f32[8,128]{1,0:T(8,128)} %param.37) | copy-start | bytes 12292
  617.6 100.7 %copy-start.45 = (f32[8,128]{1,0:T(8,128)S(1)}, f32[8,128]{1,0:T(8,128)}, u32[]{:S(2)}) copy-start(f32[8,128]{1,0:T(8,128)} %param.51) | copy-start | bytes 12292
  617.6 100.7 %copy-start.46 = (f32[8,128]{1,0:T(8,128)S(1)}, f32[8,128]{1,0:T(8,128)}, u32[]{:S(2)}) copy-start(f32[8,128]{1,0:T(8,128)} %param.44) | copy-start | bytes 12292
  617.6 269.7 %copy-start.22 = (f32[128,1024]{1,0:T(8,128)S(1)}, f32[128,1024]{1,0:T(8,128)}, u32[]{:S(2)}) copy-start(f32[128,1024]{1,0:T(8,128)} %param.34) | copy-start | bytes 1572868
  617.7 269.7 %copy-start.32 = (f32[128,1024]{1,0:T(8,128)S(1)}, f32[128,1024]{1,0:T(8,128)}, u32[]{:S(2)}) copy-start(f32[128,1024]{1,0:T(8,128)} %param.48) | copy-start | bytes 1572868
  (50 other events, 202.6 us)
Sparse Core Ops, SparseCore 0:
  10.8 46.8 all-gather.4
  126.9 49.2 all-reduce.7
  179.1 49.3 all-gather.6
  248.7 86.8 reduce-scatter.12
  338.8 50.8 all-gather.8
  402.3 49.5 all-reduce.9
  508.3 85.7 all-reduce.11
  597.5 64.1 reduce-scatter.8
  665.7 52.5 reduce-scatter.14
  722.2 74.0 reduce-scatter.6
  800.3 87.0 reduce-scatter.10
where the time goes:
time: 905 us; the launch traced here: 897 us
  waiting for transfers between devices  559 us (62%)
  blocking collectives  131 us (14%)
  matrix products  95.8 us (11%)
  other arithmetic  65 us (7%)
  local copies, waits for them, and re-layouts  23.4 us (3%)
  between operations  14.9 us (2%)
    reduce_scatter x1, waiting for transfers between devices, shards(): lax.psum_scatter(grad_expand, 'dp', scatter_dimension=0, tiled=True)  88 us
    reduce_scatter x1, waiting for transfers between devices, shards(): lax.psum_scatter(grad_shrink, 'dp', scatter_dimension=1, tiled=True)  86.9 us
    psum x1, waiting for transfers between devices, shards(): lax.psum(jnp.dot(activation, shrink_w, preferred_element_type=wide).astyp...  81.6 us
    reduce_scatter x1, waiting for transfers between devices, shards(): lax.psum_scatter(grad_heads, 'dp', scatter_dimension=1, tiled=True)  76.6 us
    reduce_scatter x1, waiting for transfers between devices, shards(): lax.psum_scatter(grad_vector, 'dp', scatter_dimension=1, tiled=True)  54.3 us
    all_gather x1, waiting for transfers between devices, shards(): lax.all_gather(param_shrink.astype(narrow), 'dp', axis=1, tiled=True)  50.7 us
    all_gather x1, waiting for transfers between devices, shards(): lax.all_gather(param_expand.astype(narrow), 'dp', axis=0, tiled=True)  45.8 us
    psum x1, waiting for transfers between devices, shards(): lax.psum(partial_two.astype(jnp.bfloat16), 'tensor').astype(jnp.float32)  43.8 us
  transfers between devices with their start and end apart: 11, of which 9 were waited for; matrix products, arithmetic and copies ran while one was open for 7% of the time, Pallas kernels for 0%

commit v1 on v0

v1 whole, which is shorter than its diff:
```python
import functools

import jax
import jax.numpy as jnp
from jax import lax
from jax.experimental import pallas as pl
from jax.experimental.pallas import tpu as pltpu
from jax.sharding import PartitionSpec as P

MESH = pl.DeviceIdType.MESH
WIDE, NARROW = jnp.float32, jnp.bfloat16

HEAD = 64
BLOCK = 256
WINDOW = 768
SMALL_ROWS = 16
VMEM_LIMIT = 66 * 1024 * 1024
LANES = 128

NORM_EPS = 1e-06
NEGATIVE = -1e30
INV_ROOT_TAU = 0.3989422804014327
BETA_ONE = 0.9
BETA_TWO = 0.999
ADAM_EPS = 1e-08
WEIGHT_DECAY = 0.05
CORRECT_ONE = 0.9999734386011124
CORRECT_TWO = 0.0952078528862904

HA, HB, MIX, EXP, SHR = 0, 1, 2, 3, 4

PLAN = {
    "start": [("begin", HB)],
    "cast": [("own", EXP)],
    "small": [("step", HA, 1)],
    "norm0": [("begin", MIX)],
    "norm1": [("step", HA, 2)],
    "norm2": [("step", HB, 1), ("step", MIX, 1)],
    "norm3": [("step", HA, 3), ("begin", EXP), ("step", HB, 2)],
    "mine": [("own", HB)],
    "first0": [("step", MIX, 2)],
    "one0": [("step", HB, 3)],
    "one1": [("own", MIX), ("step", MIX, 3), ("step", EXP, 1)],
    "one2": [("turn", EXP)],
    "two0": [("begin", SHR)],
    "two1": [("own", SHR), ("step", EXP, 2), ("late", EXP, 1)],
    "two2": [("step", EXP, 3), ("step", SHR, 1)],
    "two3": [("late", EXP, 2), ("turn", SHR)],
    "z2": [("late", EXP, 3), ("step", SHR, 2)],
    "expand1": [("late", SHR, 1), ("step", SHR, 3)],
    "expand2": [("late", SHR, 2)],
    "shrink2": [("late", SHR, 3)],
    "grow0": [("on", SHR, 1)],
    "grow2": [("leave", EXP, 0)],
    "grow3": [("on", SHR, 2)],
    "back0": [("on", SHR, 3), ("leave", EXP, 1), ("leave", EXP, 2)],
    "back1": [("leave", EXP, 3)],
    "back2": [("on", EXP, 1)],
    "back3": [("on", EXP, 2)],
    "heads": [("on", EXP, 3), ("on", MIX, 1), ("on", MIX, 2)],
    "y": [("on", MIX, 3), ("on", HA, 1), ("on", HB, 1), ("on", HA, 2), ("on", HB, 2)],
    "dx": [("on", HA, 3), ("on", HB, 3)],
    "pack": [("end", SHR), ("end", EXP)],
    "last": [("end", MIX), ("end", HA), ("end", HB)],
}


def dot(a, b):
    return jnp.dot(a, b, preferred_element_type=WIDE)


def dot_nt(a, b):
    return lax.dot_general(a, b, (((1,), (1,)), ((), ())), preferred_element_type=WIDE)


def dot_tn(a, b):
    return lax.dot_general(a, b, (((0,), (0,)), ((), ())), preferred_element_type=WIDE)


def loop(count, body):
    lax.fori_loop(0, count, lambda i, _: (body(i), None)[1], None)


def normalize(stream):
    center = stream - jnp.mean(stream, -1, keepdims=True)
    inverse = lax.rsqrt(jnp.mean(center * center, -1, keepdims=True) + NORM_EPS)
    return center * inverse, inverse


def norm_back(grad, gain, unit, inverse):
    scaled = grad * gain
    return inverse * (
        scaled - jnp.mean(scaled, -1, keepdims=True) - unit * jnp.mean(scaled * unit, -1, keepdims=True)
    )


def gelu_parts(u):
    bell = jnp.exp(-0.5 * u * u)
    base = 1.0 + (0.3275911 * 0.7071067811865476) * jnp.abs(u)
    t = pl.reciprocal(base, approx=True)
    t = t * (2.0 - base * t)
    poly = t * (
        0.5 * 0.254829592
        + t * (-0.5 * 0.284496736 + t * (0.5 * 1.421413741 + t * (-0.5 * 1.453152027 + t * (0.5 * 1.061405429))))
    )
    tail = poly * bell
    cdf = jnp.where(u >= 0, 1.0 - tail, tail)
    return u * cdf, cdf + u * bell * INV_ROOT_TAU


def fold(x):
    return jnp.sum(x.reshape(x.shape[0] // 8, 8, x.shape[1]), 0)


def kernel(
    nd,
    nt,
    tokens,
    seg_row,
    cotangent,
    own_qkv,
    own_mix,
    own_exp,
    own_shr,
    own_vec,
    own_bias,
    own_off,
    out_y,
    out_dx,
    out_ha,
    out_hb,
    out_mix,
    out_exp,
    out_shr,
    out_small,
    l_mix,
    l_shr,
    w_ha,
    w_hb,
    w_mix,
    w_exp,
    w_shr,
    z1,
    dm,
    x_own,
    c_own,
    seg_col,
    vec,
    bias,
    n1,
    r1,
    q,
    k,
    v,
    kt,
    vt,
    probs,
    inv,
    ot,
    o,
    acc,
    x1,
    att,
    n2,
    r2,
    z2,
    h,
    slope,
    da,
    ds,
    q_split,
    do_split,
    dqkv,
    dk,
    dv,
    comb,
    sums,
    bias_sums,
    row_own,
    sb,
    rb1,
    s2,
    rb2,
    m_acc,
    m_sb,
    m_rb1,
    m_s2,
    m_rb2,
    g_ha,
    g_hb,
    g_mix,
    g_exp,
    g_shr,
    p_ha,
    p_hb,
    p_mix,
    p_exp,
    p_shr,
    f_ha,
    f_hb,
    f_mix,
    f_exp,
    f_shr,
    small_in,
    vec_parts,
    small_send,
    small_recv,
    local_sem,
    ag_rs,
    ag_rr,
    ag_ls,
    ag_lr,
    ag_brs,
    ag_brr,
    ag_bls,
    ag_blr,
    ag_xs,
    ag_xr,
    rs_zs,
    rs_zr,
    rs_xs,
    rs_xr,
    sm_s,
    sm_r,
    gs_s,
    gs_r,
    vs_s,
    vs_r,
    red_s,
    red_r,
    gat_s,
    gat_r,
):
    T, D = z1.shape
    C = q.shape[1]
    F = h.shape[1]
    no = nd // 2
    cs = D // nd
    heads = C // HEAD
    blocks = D // BLOCK
    pairs = BLOCK // (2 * cs)
    own = T // nt

    me = lax.axis_index("dp")
    t = lax.axis_index("tensor")
    mz = me // 2
    mx = me % 2
    x_peer = me + 1 - 2 * mx
    mate = t + 1 - 2 * (t % 2)
    cross = (t + 2) % nt
    far = mate + 2 - 4 * (mate // 2)

    weights = (w_ha, w_hb, w_mix, w_exp, w_shr)
    grads = (g_ha, g_hb, g_mix, g_exp, g_shr)
    firsts = (p_ha, p_hb, p_mix, p_exp, p_shr)
    seconds = (f_ha, f_hb, f_mix, f_exp, f_shr)
    finals = (out_ha, out_hb, out_mix, out_exp, out_shr)
    half = C // 2
    width = 3 * half

    def rows_of(i):
        return pl.ds(pl.multiple_of(i * own, own), own)

    def chunk(ref, i):
        return ref.at[:, pl.ds(pl.multiple_of(i * cs, cs), cs), :]

    def to_dp(src, dst, send, recv, peer):
        return pltpu.make_async_remote_copy(
            src_ref=src, dst_ref=dst, send_sem=send, recv_sem=recv, device_id={"dp": peer}, device_id_type=MESH
        )

    def to_tensor(src, dst, send, recv, peer):
        return pltpu.make_async_remote_copy(
            src_ref=src, dst_ref=dst, send_sem=send, recv_sem=recv, device_id={"tensor": peer}, device_id_type=MESH
        )

    def load(i, src, dst):
        return pltpu.make_async_copy(src, dst, local_sem.at[i])

    loads = [
        load(0, own_mix, l_mix),
        load(1, own_exp, x1.at[0:cs, :]),
        load(2, own_shr, l_shr),
        load(3, tokens, z1),
        load(4, tokens.at[rows_of(t), :], x_own),
        load(5, cotangent, dm),
        load(6, cotangent.at[rows_of(t), :], c_own),
        *[load(7 + j, own_qkv.at[j], att.at[0:cs, j * C : (j + 1) * C]) for j in range(3)],
    ]
    for copy in loads[7:] + loads[:7]:
        copy.start()

    barrier = pltpu.get_barrier_semaphore()

    def greet_dp(i):
        pl.semaphore_signal(barrier, inc=1, device_id={"dp": (me + 1 + i) % nd}, device_id_type=MESH)

    def greet_tensor(i):
        pl.semaphore_signal(barrier, inc=1, device_id={"tensor": (t + 1 + i) % nt}, device_id_type=MESH)

    loop(nd - 1, greet_dp)
    loop(nt - 1, greet_tensor)

    small_in[me] = jnp.zeros_like(small_in[me])
    small_in[me, 0:8, 0:cs] = own_vec[...].astype(NARROW).astype(WIDE)
    small_in[me, 8:10, 0 : own_bias.shape[1]] = own_bias[...].astype(NARROW).astype(WIDE)
    small_in[me, 10:11, 0 : own_off.shape[1]] = own_off[...].astype(NARROW).astype(WIDE)
    for copy in loads[7:]:
        copy.wait()
    mine = pl.ds(pl.multiple_of(me * cs, cs), cs)
    for p in range(2):
        for j in range(3):
            own_part = att[0:cs, j * C + p * half : j * C + (p + 1) * half]
            weights[p][0, mine, j * half : (j + 1) * half] = own_part.astype(NARROW)
    loads[0].wait()
    w_mix[0, mine, :] = l_mix[...].T.astype(NARROW)

    pl.semaphore_wait(barrier, nd + nt - 2)

    turned = (0, 0, 0, F // 4, F // 4)

    def columns(a, i, late):
        width = weights[a].shape[2]
        split = width - turned[a]
        lanes = pl.ds(split, turned[a]) if late else pl.ds(0, split)
        return weights[a].at[:, pl.ds(pl.multiple_of(i * cs, cs), cs), lanes]

    def ag_own(a):
        slot = chunk(weights[a], me)
        return to_dp(slot, slot, ag_xs.at[a, mz], ag_xr.at[a, mz], x_peer)

    def ag_x(a, source):
        slot = columns(a, source * 2 + mx, False)
        return to_dp(slot, slot, ag_xs.at[a, source], ag_xr.at[a, source], x_peer)

    def ag_right(a, d, late=False):
        source = (mz + no + 1 - d) % no
        slot = columns(a, source * 2 + 1 - mx, True) if late else chunk(weights[a], source * 2 + mx)
        send, recv = (ag_brs, ag_brr) if late else (ag_rs, ag_rr)
        return to_dp(slot, slot, send.at[a, d], recv.at[a, d], ((mz + 1) % no) * 2 + mx)

    def ag_left(a, d, late=False):
        source = (mz + d - 1) % no
        slot = columns(a, source * 2 + 1 - mx, True) if late else chunk(weights[a], source * 2 + mx)
        send, recv = (ag_bls, ag_blr) if late else (ag_ls, ag_lr)
        return to_dp(slot, slot, send.at[a, d], recv.at[a, d], ((mz + no - 1) % no) * 2 + mx)

    def ag_leave(a, late):
        @pl.when(mz + 1 < no)
        def _():
            ag_right(a, 1, late).start()

        @pl.when(mz > 0)
        def _():
            ag_left(a, 1, late).start()

    def ag_begin(a):
        ag_leave(a, False)

    def ag_turn(a):
        ag_own(a).wait_recv()
        ag_leave(a, True)

    def ag_step(a, d, late=False):
        @pl.when(mz >= d)
        def _():
            ag_right(a, d, late).wait_recv()

            @pl.when(mz + 1 < no)
            def _():
                ag_right(a, d + 1, late).start()

            if not late:
                ag_x(a, mz - d).start()

        @pl.when(mz + d < no)
        def _():
            ag_left(a, d, late).wait_recv()

            @pl.when(mz > 0)
            def _():
                ag_left(a, d + 1, late).start()

            if not late:
                ag_x(a, mz + d).start()

    def thirds(j, body):
        low, high = 1 + (j - 1) * (no - 1) // 3, 1 + j * (no - 1) // 3
        lax.fori_loop(low, high, lambda i, _: (body(i), None)[1], None)

    def ag_third(a, j, late=False):
        if turned[a] or not late:
            thirds(j, lambda d: ag_step(a, d, late))

    def ag_finish(a):
        if not turned[a]:
            ag_own(a).wait_recv()
        peers(lambda i: ag_x(a, (mz + i) % no).wait_recv())

    def peers(body):
        loop(no - 1, lambda i: body(i + 1))

    def rs_x(a, zz):
        return to_dp(
            chunk(grads[a], zz * 2 + 1 - mx), firsts[a].at[zz], rs_xs.at[a, zz], rs_xr.at[a, zz], x_peer
        )

    def rs_z(a, kk):
        zz = (mz + kk) % no
        return to_dp(firsts[a].at[zz], seconds[a].at[kk - 1], rs_zs.at[a, kk], rs_zr.at[a, kk], zz * 2 + mx)

    def add_step(width):
        return min(cs, 128 if width <= 256 else 32)

    def rs_forward(a, kk):
        zz = (mz + kk) % no
        rs_x(a, zz).wait_recv()
        here = chunk(grads[a], zz * 2 + mx)
        step = add_step(here.shape[2])

        def add(c):
            r = pl.ds(pl.multiple_of(c * step, step), step)
            total = here[0, r, :].astype(WIDE) + firsts[a][zz, 0, r, :].astype(WIDE)
            firsts[a][zz, 0, r, :] = total.astype(NARROW)

        loop(cs // step, add)
        rs_z(a, kk).start()

    def rs_third(a, j):
        thirds(j, lambda kk: rs_forward(a, kk))

    def rs_finish(a):
        rs_x(a, mz).wait_recv()
        loop(no - 1, lambda i: rs_z(a, i + 1).wait_recv())
        here = chunk(grads[a], me)
        step = add_step(here.shape[2])

        def add(c):
            r = pl.ds(pl.multiple_of(c * step, step), step)
            total = here[0, r, :].astype(WIDE) + firsts[a][mz, 0, r, :].astype(WIDE)
            if no <= 4:
                for kk in range(no - 1):
                    total = total + seconds[a][kk, 0, r, :].astype(WIDE)
            else:
                total = lax.fori_loop(
                    0, no - 1, lambda kk, partial: partial + seconds[a][kk, 0, r, :].astype(WIDE), total
                )
            finals[a][0, r, :] = total

        loop(cs // step, add)

    def grad_block_done(a, b):
        loop(pairs, lambda j: rs_x(a, b * pairs + j).start())

    def grad_order(s):
        return (mz // pairs + 1 + s) % blocks

    steps = {
        "begin": ag_begin,
        "own": lambda a: ag_own(a).start(),
        "step": ag_third,
        "turn": ag_turn,
        "late": lambda a, j: ag_third(a, j, True),
        "leave": lambda a, j: grad_block_done(a, grad_order(j)),
        "on": rs_third,
        "end": rs_finish,
    }

    def due(place):
        for name, *args in PLAN.get(place, ()):
            steps[name](*args)

    def due_at(place, s):
        for j in range(nt):
            if place + str(j) in PLAN:

                @pl.when(s == j)
                def _():
                    due(place + str(j))

    bufs = ((sb, rb1, s2, rb2, acc), (m_sb, m_rb1, m_s2, m_rb2, m_acc))

    part_rows = own // 2

    def red(c, j):
        send, first, pair, second, _ = bufs[c]
        if j >= 2:
            rows = slice((j - 2) * part_rows, (j - 1) * part_rows)
            return to_tensor(pair.at[rows, :], second.at[rows, :], red_s.at[c, j], red_r.at[c, j], cross)
        return to_tensor(send.at[j], first.at[j], red_s.at[c, j], red_r.at[c, j], mate)

    def red_block(s):
        second = (s % 2) * 1
        first_half = far + (cross - far) * second
        last_half = mate + (t - mate) * second
        return first_half + (last_half - first_half) * (s // 2)

    def red_step(c, s):
        send, first, pair, _, total = bufs[c]

        @pl.when(s == 0)
        def _():
            send[0] = total[...].astype(NARROW)
            red(c, 0).start()

        @pl.when(s == 1)
        def _():
            red(c, 0).wait_recv()
            for hh in range(2):
                rows = slice(hh * part_rows, (hh + 1) * part_rows)
                pair[rows, :] = (total[rows, :] + first[0, rows, :].astype(WIDE)).astype(NARROW)
                if c == 0:
                    red(c, 2 + hh).start()

        @pl.when(s == 2)
        def _():
            send[1] = total[...].astype(NARROW)
            red(c, 1).start()

    def red_wait(c, hh):
        if hh == 0:
            red(c, 1).wait_recv()
        red(c, 2 + hh).wait_recv()

    def red_drain(c):
        for j in range(4):
            red(c, j).wait_send()

    def red_rows(c, r):
        _, first, _, second, total = bufs[c]
        return total[r, :] + first[1, r, :].astype(WIDE) + second[r, :].astype(WIDE)

    def gat(g, src, ref, j):
        if j == 0:
            return to_tensor(src, ref.at[rows_of(t), :], gat_s.at[g, 0], gat_r.at[g, 0], mate)
        if j == 1:
            block = ref.at[rows_of(cross), :]
            return to_tensor(block, block, gat_s.at[g, 1], gat_r.at[g, 1], mate)
        rows = slice((j - 2) * part_rows, (j - 1) * part_rows)
        there = pl.ds(pl.multiple_of(t * own + (j - 2) * part_rows, part_rows), part_rows)
        return to_tensor(src.at[rows, :], ref.at[there, :], gat_s.at[g, j], gat_r.at[g, j], cross)

    def in_halves(c, g, src, ref, body):
        steps = own // 64 // 2
        for hh in range(2):
            red_wait(c, hh)
            lax.fori_loop(hh * steps, (hh + 1) * steps, lambda i, _: (body(i), None)[1], None)
            gat(g, src, ref, 2 + hh).start()
        gat(g, src, ref, 0).start()
        ref[rows_of(t), :] = src[...]
        red_drain(c)

    def gat_forward(g, src, ref):
        for hh in range(2):
            gat(g, src, ref, 2 + hh).wait_recv()
        gat(g, src, ref, 1).start()

    def small(kk):
        return to_dp(small_in.at[me], small_in.at[me], sm_s.at[kk], sm_r.at[kk], (me + kk) % nd)

    loop(nd - 1, lambda i: small(i + 1).start())
    ag_begin(HA)
    ag_own(HA).start()
    due("start")
    loads[1].wait()
    w_exp[0, mine, :] = x1[0:cs, :].astype(NARROW)
    loads[2].wait()
    w_shr[0, mine, :] = l_shr[...].T.astype(NARROW)
    due("cast")

    place = lax.broadcasted_iota(jnp.int32, (1, T), 1)
    marks = seg_row[...]
    marks = jnp.where(marks >= 0, marks, -1 - place).astype(WIDE)
    for i in range(T // LANES):
        part = marks[:, i * LANES : (i + 1) * LANES]
        seg_col[i * LANES : (i + 1) * LANES, :] = jnp.broadcast_to(part, (LANES, LANES)).T

    def marks_of(i):
        there = seg_row[:, pl.ds(pl.multiple_of(i * BLOCK, BLOCK), BLOCK)]
        at = lax.broadcasted_iota(jnp.int32, (1, BLOCK), 1) + i * BLOCK
        return jnp.where(there >= 0, there, -1 - at).astype(WIDE)

    loop(nd - 1, lambda i: small(i + 1).wait_recv())

    low = lax.broadcasted_iota(jnp.int32, (LANES, F), 0) * nd
    col = lax.broadcasted_iota(jnp.int32, (LANES, F), 1)
    comb[...] = jnp.where((col >= low) & (col < low + nd), 1.0, 0.0).astype(NARROW)
    bias[...] = jnp.zeros_like(bias)

    def of_peer(i):
        return lax.broadcasted_iota(jnp.int32, (1, F), 1) % nd == i

    def spread(i):
        bias[...] += jnp.where(of_peer(i), dot(small_in[i].astype(NARROW), comb[...]), 0.0)

    loop(nd, spread)
    if cs == LANES:
        for i in range(nd):
            vec[0:8, i * cs : (i + 1) * cs] = small_in[i, 0:8, :]
    else:
        vec[...] = jnp.zeros_like(vec)

        def spread_vec(i):
            low = lax.broadcasted_iota(jnp.int32, (LANES, D), 0)
            col = lax.broadcasted_iota(jnp.int32, (LANES, D), 1)
            pick = jnp.where(col == i * cs + low, 1.0, 0.0).astype(NARROW)
            vec[...] += dot(small_in[i].astype(NARROW), pick)

        loop(nd, spread_vec)

    due("small")

    loads[3].wait()

    def norm_one(i):
        r = pl.ds(pl.multiple_of(i * 64, 64), 64)
        unit, _ = normalize(z1[r, :].astype(WIDE))
        z1[r, :] = (unit * vec[0:1, :] + vec[1:2, :]).astype(NARROW)

    quarter = T // 64 // 4

    def norm_quarter(j):
        lax.fori_loop(j * quarter, (j + 1) * quarter, lambda i, _: (norm_one(i), None)[1], None)

    for j in range(4):
        norm_quarter(j)
        due("norm" + str(j))

    loads[4].wait()

    def norm_own(i):
        r = pl.ds(pl.multiple_of(i * 64, 64), 64)
        unit, inverse = normalize(x_own[r, :].astype(WIDE))
        n1[r, :] = unit
        r1[r, :] = inverse

    loop(own // 64, norm_own)
    due("mine")

    loads[5].wait()
    loads[6].wait()

    def scale_cot(i):
        r = pl.ds(pl.multiple_of(i * 64, 64), 64)
        dm[r, :] = (dm[r, :].astype(WIDE) * vec[7:8, :]).astype(NARROW)

    loop(T // 64, scale_cot)
    ag_finish(HA)

    scaling = HEAD ** (-0.5)

    def project(p, i):
        r = pl.ds(pl.multiple_of(i * BLOCK, BLOCK), BLOCK)
        here = slice(p * half, (p + 1) * half)
        three = dot(z1[r, :], weights[p][0])
        query = (three[:, 0:half] + bias[8:9, here]).astype(NARROW)
        q[r, here] = (query.astype(WIDE) * scaling).astype(NARROW)
        key = three[:, half : 2 * half].astype(NARROW)
        k[r, here] = key
        value = (three[:, 2 * half :] + bias[9:10, here]).astype(NARROW)
        v[r, here] = value
        kt[here, r] = key.T
        vt[here, r] = value.T

    def head_rows(x, hh):
        parts = []
        if hh > 0:
            parts.append(jnp.zeros((hh * HEAD, x.shape[1]), x.dtype))
        parts.append(x[hh * HEAD : (hh + 1) * HEAD, :])
        if (hh + 1) * HEAD < x.shape[0]:
            parts.append(jnp.zeros((x.shape[0] - (hh + 1) * HEAD, x.shape[1]), x.dtype))
        return jnp.concatenate(parts, 0)

    def window(i):
        return pl.ds(pl.multiple_of((i // 2) * BLOCK, BLOCK), WINDOW)

    def part(i, c):
        return pl.ds(pl.multiple_of((i // 2) * BLOCK + c * LANES, LANES), LANES)

    parts = WINDOW // LANES
    mask = dk

    def score_place(hh, c):
        if hh % 2 == 0:
            return dv.at[c * LANES : (c + 1) * LANES, :]
        return m_acc.at[(c % 2) * LANES : (c % 2 + 1) * LANES, (c // 2) * BLOCK : (c // 2 + 1) * BLOCK]

    def attend(p, s):
        i = red_block(s)
        r = rows_of(i)
        w = window(i)
        here = marks_of(i)
        mine = slice(p * half, (p + 1) * half)
        for c in range(parts):
            keys = seg_col[part(i, c), :]
            keys = jnp.concatenate([keys, keys], 1)
            mask[c * LANES : (c + 1) * LANES, :] = jnp.where(keys == here, 0.0, NEGATIVE)
        qt = q[r, mine].T
        count = heads // 2
        highest, mixed = [None] * count, [None] * count

        def score(hh):
            queries = head_rows(qt, hh)
            top = None
            for c in range(parts):
                scores = dot(k[part(i, c), mine], queries) + mask[c * LANES : (c + 1) * LANES, :]
                score_place(hh, c)[...] = scores
                most = jnp.max(scores.reshape(LANES // 8, 8, BLOCK), 0)
                top = most if top is None else jnp.maximum(top, most)
            highest[hh] = jnp.max(top, 0, keepdims=True)

        def mix(hh):
            head = p * count + hh
            cols = slice(head * BLOCK, (head + 1) * BLOCK)
            total = jnp.zeros((8, BLOCK), WIDE)
            for c in range(parts):
                expo = jnp.exp(score_place(hh, c)[...] - highest[hh])
                total = total + fold(expo)
                probs[i, c * LANES : (c + 1) * LANES, cols] = expo.astype(NARROW)
            inverse = 1.0 / jnp.sum(total, 0, keepdims=True)
            inv[i, head : head + 1, :] = inverse
            mixed[hh] = dot(vt[head * HEAD : (head + 1) * HEAD, w], probs[i, :, cols]) * inverse

        score(0)
        for hh in range(1, count):
            score(hh)
            mix(hh - 1)
        mix(count - 1)
        mixed = jnp.concatenate(mixed, 0)
        ot[i, mine, :] = mixed
        o[r, mine] = mixed.astype(NARROW).T

    def project_two(p, j, place):
        lax.fori_loop(2 * j, 2 * j + 2, lambda i, _: (project(p, i), None)[1], None)
        due(place + str(j))

    def attend_one(s):
        attend(0, s)
        due_at("one", s)

    def attend_two(s):
        attend(1, s)

        @pl.when(s == 0)
        def _():
            ag_finish(MIX)

        acc[...] = dot_nt(o[rows_of(red_block(s)), :], w_mix[0])
        red_step(0, s)
        due_at("two", s)

    for j in range(2):
        project_two(0, j, "first")
    loop(nt, attend_one)
    ag_finish(HB)
    for j in range(2):
        project_two(1, j, "second")
    loop(nt, attend_two)

    def middle(i):
        r = pl.ds(pl.multiple_of(i * 64, 64), 64)
        a = red_rows(0, r) + vec[2:3, :]
        att[r, :] = a
        x = x_own[r, :].astype(WIDE) + vec[3:4, :] * a
        x1[r, :] = x
        unit, inverse = normalize(x)
        n2[r, :] = unit
        r2[r, :] = inverse
        row_own[r, :] = (unit * vec[4:5, :] + vec[5:6, :]).astype(NARROW)

    in_halves(0, 0, row_own, z2, middle)
    due("z2")
    ag_finish(EXP)

    def tile(n):
        return slice(n * BLOCK, (n + 1) * BLOCK)

    def in_tiles(count, product, act):
        product(0)
        for n in range(1, count):
            product(n)
            act(n - 1)
        act(count - 1)

    def gat_wait(g, src, ref, s):
        @pl.when(s == 1)
        def _():
            gat(g, src, ref, 0).wait_recv()

        @pl.when(s == 2)
        def _():
            gat_forward(g, src, ref)

        @pl.when(s == 3)
        def _():
            gat(g, src, ref, 1).wait_recv()

    def expand(s):
        gat_wait(0, row_own, z2, s)
        i = red_block(nt - 1 - s)
        r = rows_of(i)

        def product(n):
            acc[:, tile(n)] = dot(z2[r, :], w_exp[0, :, tile(n)])

        def act(n):
            for c in range(own // 32):
                there = pl.ds(pl.multiple_of(i * own + c * 32, 32), 32)
                value, rise = gelu_parts(acc[c * 32 : (c + 1) * 32, tile(n)] + bias[10:11, tile(n)])
                h[there, tile(n)] = value.astype(NARROW)
                slope[there, tile(n)] = rise.astype(NARROW)

        in_tiles(F // BLOCK, product, act)

        due_at("expand", s)

    loop(nt, expand)

    def grad_shrink(s):
        b = grad_order(s)
        cols = pl.ds(pl.multiple_of(b * BLOCK, BLOCK), BLOCK)
        g_shr[0, cols, :] = dot_tn(dm[:, cols], h[...]).astype(NARROW)
        grad_block_done(SHR, b)
        due_at("shrink", s)

    loop(blocks, grad_shrink)
    ag_finish(SHR)

    bias_sums[...] = jnp.zeros_like(bias_sums)
    sums[...] = jnp.zeros_like(sums)

    def back(s):
        i = red_block(s)
        r = rows_of(i)

        def product(n):
            acc[:, tile(n)] = dot(dm[r, :], w_shr[0, :, tile(n)])

        def act(n):
            total = jnp.zeros((8, BLOCK), WIDE)
            for c in range(own // 32):
                there = pl.ds(pl.multiple_of(i * own + c * 32, 32), 32)
                du = acc[c * 32 : (c + 1) * 32, tile(n)] * slope[there, tile(n)].astype(WIDE)
                du = du.astype(NARROW)
                slope[there, tile(n)] = du
                total = total + fold(du.astype(WIDE))
            bias_sums[16:24, tile(n)] += total

        in_tiles(F // BLOCK, product, act)
        for n in range(D // BLOCK):
            acc[:, tile(n)] = dot_nt(slope[r, :], w_exp[0, tile(n), :])
        red_step(0, s)

    loop(nt, back)

    def grad_expand(s):
        b = grad_order(s)
        cols = pl.ds(pl.multiple_of(b * BLOCK, BLOCK), BLOCK)
        g_exp[0, cols, :] = dot_tn(z2[:, cols], slope[...]).astype(NARROW)

        due_at("grow", s)

    loop(blocks, grad_expand)

    for j in range(4):
        gat(0, row_own, z2, j).wait_send()

    def middle_back(i):
        r = pl.ds(pl.multiple_of(i * 64, 64), 64)
        grad = red_rows(0, r)
        unit = n2[r, :]
        sums[4 * 8 : 5 * 8, :] += fold(grad * unit)
        sums[5 * 8 : 6 * 8, :] += fold(grad)
        dx1 = c_own[r, :].astype(WIDE) + norm_back(grad, vec[4:5, :], unit, r2[r, :])
        sums[3 * 8 : 4 * 8, :] += fold(dx1 * att[r, :])
        n2[r, :] = dx1
        grad_att = (vec[3:4, :] * dx1).astype(NARROW)
        row_own[r, :] = grad_att
        sums[2 * 8 : 3 * 8, :] += fold(grad_att.astype(WIDE))

    in_halves(0, 1, row_own, da, middle_back)

    def shrink(s):
        r = rows_of(red_block(s))
        m_acc[...] = dot_nt(h[r, :], w_shr[0])
        red_step(1, s)

    dk[...] = jnp.zeros_like(dk)
    dv[...] = jnp.zeros_like(dv)
    lane = lax.broadcasted_iota(jnp.int32, (1, C), 1)

    def grad_mix(s):
        b = grad_order(s)
        cols = pl.ds(pl.multiple_of(b * BLOCK, BLOCK), BLOCK)
        g_mix[0, cols, :] = dot_tn(da[:, cols], o[...]).astype(NARROW)
        grad_block_done(MIX, b)

    def attend_back(s):
        @pl.when(s == 2)
        def _():
            loop(nt, shrink)

        gat_wait(1, row_own, da, s)

        @pl.when(s == 2)
        def _():
            red(1, 2).start()
            red(1, 3).start()

        @pl.when(s == 3)
        def _():
            loop(blocks, grad_mix)

        i = red_block(nt - 1 - s)
        r = rows_of(i)
        w = window(i)
        do = dot(da[r, :], w_mix[0]).astype(NARROW)
        dot_ = do.T.astype(WIDE)
        whole = []
        for hh in range(heads):
            whole.append(jnp.broadcast_to(inv[i, hh : hh + 1, :], (HEAD, BLOCK)))
        scaled = dot_ * jnp.concatenate(whole, 0)
        delta = scaled * ot[i]
        scaled_t = scaled.astype(NARROW)
        natural = scaled_t.T.astype(WIDE)
        queries = q[r, :].astype(WIDE)
        back_q = []

        def grad_scores(hh):
            cols = slice(hh * BLOCK, (hh + 1) * BLOCK)
            here = (lane >= hh * HEAD) & (lane < (hh + 1) * HEAD)
            q_split[cols, :] = jnp.where(here, queries, 0.0).astype(NARROW)
            do_split[cols, :] = jnp.where(here, natural, 0.0).astype(NARROW)
            shift = jnp.sum(delta[hh * HEAD : (hh + 1) * HEAD, :], 0, keepdims=True)
            grads_o = head_rows(scaled_t, hh)
            for c in range(parts):
                place = slice(c * LANES, (c + 1) * LANES)
                grad_p = dot(v[part(i, c), :], grads_o)
                ds[place, cols] = (probs[i, place, cols].astype(WIDE) * (grad_p - shift)).astype(NARROW)

        def grad_queries(hh):
            cols = slice(hh * BLOCK, (hh + 1) * BLOCK)
            back_q.append(dot(kt[hh * HEAD : (hh + 1) * HEAD, w], ds[:, cols]))

        grad_scores(0)
        for hh in range(1, heads):
            grad_scores(hh)
            grad_queries(hh - 1)
        grad_queries(heads - 1)
        grad_q = (jnp.concatenate(back_q, 0) * scaling).astype(NARROW).T
        dqkv[r, 0:half] = grad_q[:, 0:half]
        dqkv[r, width : width + half] = grad_q[:, half:C]
        for c in range(WINDOW // BLOCK):
            place = slice(c * BLOCK, (c + 1) * BLOCK)
            there = pl.ds(pl.multiple_of((i // 2) * BLOCK + c * BLOCK, BLOCK), BLOCK)
            dk[there, :] += dot(ds[place, :], q_split[...])
            dv[there, :] += dot(probs[i, place, :], do_split[...])

        due_at("back", s)

    loop(nt, attend_back)

    def round_kv(i):
        r = pl.ds(pl.multiple_of(i * 128, 128), 128)
        grad_k = dk[r, :].astype(NARROW)
        grad_v = dv[r, :].astype(NARROW)
        for p in range(2):
            here = slice(p * half, (p + 1) * half)
            dqkv[r, p * width + half : p * width + 2 * half] = grad_k[:, here]
            dqkv[r, p * width + 2 * half : (p + 1) * width] = grad_v[:, here]
            bias_sums[0:8, here] += fold(dqkv[r, p * width : p * width + half].astype(WIDE))
        bias_sums[8:16, 0:C] += fold(grad_v.astype(WIDE))

    loop(T // 128, round_kv)

    def grad_qkv(s):
        b = grad_order(s)
        cols = pl.ds(pl.multiple_of(b * BLOCK, BLOCK), BLOCK)
        both = dot_tn(z1[:, cols], dqkv[...]).astype(NARROW)
        for p in range(2):
            grads[p][0, cols, :] = both[:, p * width : (p + 1) * width]
            grad_block_done(p, b)

    def first_back(s):
        r = rows_of(red_block(s))
        acc[...] = dot_nt(dqkv[r, 0:width], w_ha[0]) + dot_nt(dqkv[r, width : 2 * width], w_hb[0])
        red_step(0, s)

    loop(nt, first_back)
    loop(blocks, grad_qkv)
    due("heads")

    for j in range(4):
        gat(1, row_own, da, j).wait_send()

    def finish_y(i):
        r = pl.ds(pl.multiple_of(i * 64, 64), 64)
        m = red_rows(1, r) + vec[6:7, :]
        dy = c_own[r, :].astype(WIDE)
        sums[7 * 8 : 8 * 8, :] += fold(dy * m)
        sums[6 * 8 : 7 * 8, :] += fold((vec[7:8, :] * dy).astype(NARROW).astype(WIDE))
        row_own[r, :] = (x1[r, :] + vec[7:8, :] * m).astype(NARROW)

    in_halves(1, 2, row_own, dm, finish_y)

    due("y")
    def finish_dx(i):
        r = pl.ds(pl.multiple_of(i * 64, 64), 64)
        grad = red_rows(0, r)
        unit = n1[r, :]
        sums[0 * 8 : 1 * 8, :] += fold(grad * unit)
        sums[1 * 8 : 2 * 8, :] += fold(grad)
        dx = n2[r, :] + norm_back(grad, vec[0:1, :], unit, r1[r, :])
        x_own[r, :] = dx.astype(NARROW)

    in_halves(0, 3, x_own, z2, finish_dx)
    due("dx")

    for j in range(8):
        vec_parts[t, j : j + 1, :] = jnp.sum(sums[j * 8 : (j + 1) * 8, :], 0, keepdims=True)

    def vec_to(kk):
        return to_tensor(vec_parts.at[t], vec_parts.at[t], vs_s.at[kk], vs_r.at[kk], (t + kk) % nt)

    loop(nt - 1, lambda i: vec_to(i + 1).start())
    gat_forward(2, row_own, dm)
    loop(nt - 1, lambda i: vec_to(i + 1).wait_recv())
    total = vec_parts[0]
    for j in range(1, nt):
        total = total + vec_parts[j]
    lines = [jnp.sum(bias_sums[j * 8 : (j + 1) * 8, :], 0, keepdims=True) for j in range(3)]
    lines = jnp.concatenate(lines + [jnp.zeros((5, F), WIDE)], 0)
    high = lines.astype(NARROW).astype(WIDE)
    lines = jnp.concatenate([high, lines - high], 0)

    def pack(i):
        both = dot_nt(jnp.where(of_peer(i), lines, 0.0).astype(NARROW), comb[...])
        small_send[i, 8:16, :] = both[0:8, :] + both[8:16, :]

    loop(nd, pack)
    if cs == LANES:
        for i in range(nd):
            small_send[i, 0:8, :] = total[:, i * cs : (i + 1) * cs]
    else:
        vec_high = total.astype(NARROW)
        vec_low = (total - vec_high.astype(WIDE)).astype(NARROW)

        def pack_vec(i):
            row = lax.broadcasted_iota(jnp.int32, (D, LANES), 0)
            low = lax.broadcasted_iota(jnp.int32, (D, LANES), 1)
            pick = jnp.where((row == i * cs + low) & (low < cs), 1.0, 0.0).astype(NARROW)
            small_send[i, 0:8, :] = dot(vec_high, pick) + dot(vec_low, pick)

        loop(nd, pack_vec)

    def grad_small(kk):
        peer = (me + kk) % nd
        return to_dp(small_send.at[peer], small_recv.at[me], gs_s.at[kk], gs_r.at[kk], peer)

    loop(nd - 1, lambda i: grad_small(i + 1).start())
    small_recv[me] = small_send[me]
    due("pack")
    gat_forward(3, x_own, z2)
    due("last")
    loop(nd - 1, lambda i: grad_small(i + 1).wait_recv())
    out_small[...] = lax.fori_loop(
        1, nd, lambda i, s: s + small_recv[i], small_recv[0]
    )

    def ag_drain(a, d):
        for late in (False, True) if turned[a] else (False,):

            @pl.when((mz + 1 < no) & (mz + 1 >= d))
            def _():
                ag_right(a, d, late).wait_send()

            @pl.when((mz > 0) & (mz + d <= no))
            def _():
                ag_left(a, d, late).wait_send()

    keep = []
    for g, src, ref, out in ((2, row_own, dm, out_y), (3, x_own, z2, out_dx)):
        gat(g, src, ref, 0).wait_recv()
        gat(g, src, ref, 1).wait_recv()
        keep.append(load(8 + g, ref, out))
        keep[-1].start()
        for j in range(4):
            gat(g, src, ref, j).wait_send()
    for a in range(5):
        peers(functools.partial(ag_drain, a))
        ag_own(a).wait_send()
        peers(lambda i: ag_x(a, (mz + i) % no).wait_send())
        loop(no - 1, lambda i: rs_z(a, i + 1).wait_send())
        loop(no, lambda i: rs_x(a, i).wait_send())
    loop(nd - 1, lambda i: small(i + 1).wait_send())
    loop(nd - 1, lambda i: grad_small(i + 1).wait_send())
    loop(nt - 1, lambda i: vec_to(i + 1).wait_send())
    for copy in keep:
        copy.wait()


def layer(nd, nt, tokens, segments, cotangent, heads, mixer, expand, shrink, vector, biases, offset):
    T, D = tokens.shape
    C, F = heads.shape[2], expand.shape[1]
    cs, no, own = D // nd, nd // 2, T // nt
    sds = jax.ShapeDtypeStruct
    dma = pltpu.SemaphoreType.DMA

    def nar(*shape):
        return pltpu.VMEM(shape, NARROW)

    def wid(*shape):
        return pltpu.VMEM(shape, WIDE)

    shapes = ((1, 3 * C // 2), (1, 3 * C // 2), (1, C), (1, F), (1, F))
    scratch = [wid(*x.shape) for x in (mixer, shrink)]
    scratch += [nar(m, D, w) for m, w in shapes]
    scratch += [nar(T, D), nar(T, D), nar(own, D), nar(own, D), wid(T, LANES)]
    scratch += [wid(SMALL_ROWS, D), wid(SMALL_ROWS, F), wid(own, D), wid(own, 1)]
    scratch += [nar(T, C), nar(T, C), nar(T, C), nar(C, T), nar(C, T)]
    scratch += [nar(nt, WINDOW, (C // HEAD) * BLOCK)]
    scratch += [wid(nt, 8, BLOCK), wid(nt, C, BLOCK), nar(T, C), wid(own, D)]
    scratch += [wid(own, D), wid(own, D), wid(own, D), wid(own, 1)]
    scratch += [nar(T, D), nar(T, F), nar(T, F), nar(T, D)]
    scratch += [nar(WINDOW, (C // HEAD) * BLOCK), nar((C // HEAD) * BLOCK, C), nar((C // HEAD) * BLOCK, C)]
    scratch += [nar(T, 3 * C), wid(T, C), wid(T, C), nar(LANES, F)]
    scratch += [wid(64, D), wid(24, F), nar(own, D)]
    scratch += [nar(2, own, D), nar(2, own, D), nar(own, D), nar(own, D)]
    scratch += [wid(own, D), nar(2, own, D), nar(2, own, D), nar(own, D), nar(own, D)]
    scratch += [nar(m, D, w) for m, w in shapes]
    scratch += [nar(no, m, cs, w) for m, w in shapes]
    scratch += [nar(no - 1, m, cs, w) for m, w in shapes]
    scratch += [wid(nd, SMALL_ROWS, LANES), wid(nt, 8, D), wid(nd, SMALL_ROWS, LANES), wid(nd, SMALL_ROWS, LANES)]
    scratch += [dma((12,))]
    scratch += [dma((5, no + 1)) for _ in range(8)] + [dma((5, no)) for _ in range(6)]
    scratch += [dma((nd,)) for _ in range(4)]
    scratch += [dma((nt,)) for _ in range(2)]
    scratch += [dma((2, 4)), dma((2, 4)), dma((4, 4)), dma((4, 4))]

    anywhere = pl.BlockSpec(memory_space=pl.ANY)
    vmem = pl.BlockSpec(memory_space=pltpu.VMEM)
    return pl.pallas_call(
        functools.partial(kernel, nd, nt),
        out_shape=[
            sds((T, D), NARROW),
            sds((T, D), NARROW),
            *[sds((m, cs, w), WIDE) for m, w in shapes],
            sds((SMALL_ROWS, LANES), WIDE),
        ],
        in_specs=[anywhere, vmem] + [anywhere] * 5 + [vmem] * 3,
        out_specs=[anywhere, anywhere] + [vmem] * 6,
        scratch_shapes=scratch,
        compiler_params=pltpu.CompilerParams(
            collective_id=0, has_side_effects=True, vmem_limit_bytes=VMEM_LIMIT
        ),
    )(tokens, segments.reshape(1, T), cotangent, heads, mixer, expand, shrink, vector, biases, offset)


def update_kernel(*refs):
    raw_y, raw_dx = refs[:2]
    sources, refs = refs[2:29], refs[29:]
    out_y, out_dx = refs[:2]
    targets, refs = refs[2:16], refs[16:]
    held, news, t_mix, t_shr = refs[:27], refs[27:41], refs[41], refs[42]
    held_y, held_dx, sem = refs[43:]
    first = (0, 1, 6, 13, 20, 3, 9, 16, 23)
    loads = [pltpu.make_async_copy(sources[i], held[i], sem.at[i]) for i in range(27)]
    take = [
        pltpu.make_async_copy(raw_y, held_y, sem.at[27]),
        pltpu.make_async_copy(raw_dx, held_dx, sem.at[28]),
    ]
    for i in first:
        loads[i].start()
    for i in (4, 11, 18, 25, 2, 8, 15, 22):
        loads[i].start()
    for copy in take:
        copy.start()
    for i in (5, 7, 10, 12, 14, 17, 19, 21, 24, 26):
        loads[i].start()
    keep = [
        pltpu.make_async_copy(held_y, out_y, sem.at[43]),
        pltpu.make_async_copy(held_dx, out_dx, sem.at[44]),
    ]
    grads, state = held[:6], held[6:]
    stores = [pltpu.make_async_copy(news[i], targets[i], sem.at[29 + i]) for i in range(14)]

    def arrive(slot, source=None):
        if source is not None:
            loads[source].wait()
        for j in range(3):
            loads[6 + slot + 7 * j].wait()

    def update(slot, gradient, decay_rate, at=lambda ref: ref):
        master, moment, square = (at(state[slot + 7 * j])[...] for j in range(3))
        moment = BETA_ONE * moment + (1.0 - BETA_ONE) * gradient
        square = BETA_TWO * square + (1.0 - BETA_TWO) * gradient * gradient
        at(news[slot + 7])[...] = moment
        change = moment * (1 / CORRECT_ONE) / (jnp.sqrt(square * (1 / CORRECT_TWO)) + ADAM_EPS)
        at(news[slot])[...] = change + decay_rate * master

    def by_rows(slot, gradient, step):
        def one(c):
            r = pl.ds(pl.multiple_of(c * step, step), step)
            update(slot, gradient[r, :], WEIGHT_DECAY, lambda ref: ref.at[r, :])

        loop(gradient.shape[0] // step, one)

    def leave(slot):
        stores[slot].start()
        stores[slot + 7].start()

    loads[1].wait()
    arrive(0, 0)
    half = grads[0].shape[2] // 3
    for j in range(3):
        here = slice(j * half, (j + 1) * half)
        whole = jnp.concatenate([grads[0][0, :, here], grads[1][0, :, here]], 1)
        update(0, whole, WEIGHT_DECAY, lambda ref: ref.at[j])
    leave(0)
    arrive(3, 3)
    by_rows(3, grads[3].at[0], min(32, grads[3].shape[1]))
    leave(3)
    for j in range(2):
        take[j].wait()
        keep[j].start()
    arrive(5, 4)
    t_shr[...] = grads[4][0].T
    by_rows(5, t_shr, 256)
    leave(5)
    arrive(2, 2)
    t_mix[...] = grads[2][0].T
    by_rows(2, t_mix, 256)
    leave(2)
    loads[5].wait()
    small = grads[5]
    for slot, rows in ((1, slice(8, 10)), (4, slice(10, 11)), (6, slice(0, 8))):
        arrive(slot)
        update(slot, small[rows, 0 : state[slot].shape[1]], 0.0)
        leave(slot)
    for copy in keep + stores:
        copy.wait()


def shards(nd, nt, tokens, segments, cotangent, *state):
    heads, biases, mixer, expand, offset, shrink, vector = state[:7]
    flat = list(state)
    for j in range(0, 21, 7):
        flat[j + 1] = state[j + 1].reshape(2, -1)
        flat[j + 4] = state[j + 4].reshape(1, -1)
    results = layer(nd, nt, tokens, segments, cotangent, heads, mixer, expand, shrink, vector, flat[1], flat[4])
    anywhere = pl.BlockSpec(memory_space=pl.ANY)
    sds = jax.ShapeDtypeStruct
    outs = pl.pallas_call(
        update_kernel,
        out_shape=[sds(x.shape, x.dtype) for x in results[:2]] + [sds(x.shape, WIDE) for x in flat[:7]] * 2,
        in_specs=[anywhere] * 29,
        out_specs=[anywhere] * 16,
        scratch_shapes=[
            *[pltpu.VMEM(x.shape, WIDE) for x in (*results[2:], *flat, *flat[:7], *flat[:7], mixer, shrink)],
            pltpu.VMEM(results[0].shape, NARROW),
            pltpu.VMEM(results[1].shape, NARROW),
            pltpu.SemaphoreType.DMA((45,)),
        ],
        compiler_params=pltpu.CompilerParams(vmem_limit_bytes=VMEM_LIMIT),
    )(*results, *flat)
    outs = list(outs)
    for j in (2, 9):
        outs[j + 1] = outs[j + 1].reshape(biases.shape)
        outs[j + 4] = outs[j + 4].reshape(offset.shape)
    return tuple(outs)


def solution(mesh):
    matrices = (
        P(None, "dp", "tensor"),
        P(None, "tensor", "dp"),
        P("tensor", "dp"),
        P("dp", "tensor"),
        P("tensor", "dp"),
        P("tensor", "dp"),
        P(None, "dp"),
    )
    rows = P("dp", None)
    return jax.shard_map(
        functools.partial(shards, mesh.shape["dp"], mesh.shape["tensor"]),
        mesh=mesh,
        in_specs=(rows, P("dp"), rows) + matrices * 3,
        out_specs=(rows, rows) + matrices * 2,
        check_vma=False,
    )
```

time: 905 us -> 169 us (0.19)
  waiting for transfers between devices: 559 us -> 0 us
  Pallas kernels: 0 us -> 168 us
  blocking collectives: 131 us -> 0 us
  matrix products: 95.8 us -> 0 us
  other arithmetic: 65 us -> 0 us
  local copies, waits for them, and re-layouts: 23.4 us -> 0 us
  between operations: 14.9 us -> 0.81 us
    reduce_scatter x5 -> x0, waiting for transfers between devices: 306 us -> none  [the longest x1 88 us: shards(): lax.psum_scatter(grad_expand, 'dp', scatter_dimension=0, tiled=True)]
    pallas_call x0 -> x2, Pallas kernels: none -> 168 us  [the longest x1 161 us: layer(): pl.pallas_call(functools.partial(kernel, nd, nt), out_shape=[sds((T, D),...]
    psum x3 -> x0, waiting for transfers between devices: 156 us -> none  [the longest x1 81.6 us: shards(): lax.psum(jnp.dot(activation, shrink_w, preferred_element_type=wide).astyp...]
    all_gather x3 -> x0, waiting for transfers between devices: 96.6 us -> none  [the longest x1 50.7 us: shards(): lax.all_gather(param_shrink.astype(narrow), 'dp', axis=1, tiled=True)]
    dot_general x28 -> x0, matrix products: 95.8 us -> none  [the longest x1 14.3 us: shards(): jnp.dot(normed_two, expand_w, preferred_element_type=wide) + offset]
    all_gather x4 -> x0, blocking collectives: 93 us -> none  [the longest x1 28.1 us: shards(): lax.all_gather(param_mixer.astype(narrow), 'dp', axis=1, tiled=True)]
    unnamed x1 -> x0, blocking collectives: 38 us -> none
    reduce_sum x13 -> x0, other arithmetic: 32.1 us -> none  [the longest x1 7.52 us: shards(): grad_scale_two = jnp.sum(grad_out * mlp_out, 0)]
  transfers between devices with their start and end apart: 11 -> 0, of which waited for: 9 -> 0; matrix products, arithmetic and copies ran while one was open for 7% -> 0% of each run, Pallas kernels for 0% -> 0%
where the time goes in v1:
time: 169 us
  Pallas kernels  168 us (99%)
    pallas_call x1, Pallas kernels, layer(): pl.pallas_call(functools.partial(kernel, nd, nt), out_shape=[sds((T, D),...  161 us
    pallas_call x1, Pallas kernels, shards(): pl.pallas_call(update_kernel, out_shape=[sds(x.shape, x.dtype) for x in r...  7.14 us

profile of v1, /device:TPU:0, one launch (start us, length us, event | category | flops | bytes accessed | tf_op | source)
XLA Modules:
  0.0 169.0 jit_solution(15231439625550346792)
XLA Ops:
  0.6 161.0 %shard_map.351 = (bf16[1024,1024]{1,0:T(8,128)(2,1)}, bf16[1024,1024]{1,0:T(8,128)(2,1)}, f32[1,128,384]{2,1,0:T(8,128)}, f32[1,128,384]{2,1,0:T(8,128)}, f32[1,...) custom-call(bf16[1024,1024]{1,0:T(8,128)(2,1)} %tokens.1, ...), custom_call_target="tpu_custom_call" | custom-call | tf_op jit(solution)/shard_map/pallas_call | solution.py:1142
  161.7 7.1 %shard_map.352 = (bf16[1024,1024]{1,0:T(8,128)(2,1)}, bf16[1024,1024]{1,0:T(8,128)(2,1)}, f32[3,128,256]{2,1,0:T(8,128)}, f32[2,32]{1,0:T(2,128)}, f32[256,128]{...) custom-call(bf16[1024,1024]{1,0:T(8,128)(2,1)} %get-tuple-element.40, ...), custom_call_target="tpu_custom_call" | custom-call | tf_op jit(solution)/shard_map/pallas_call | solution.py:1253

commit v2 on v1

--- a/solution.py
+++ b/solution.py
@@ -907,10 +907,6 @@
             red(1, 2).start()
             red(1, 3).start()
 
-        @pl.when(s == 3)
-        def _():
-            loop(blocks, grad_mix)
-
         i = red_block(nt - 1 - s)
         r = rows_of(i)
         w = window(i)
@@ -968,8 +964,6 @@
             here = slice(p * half, (p + 1) * half)
             dqkv[r, p * width + half : p * width + 2 * half] = grad_k[:, here]
             dqkv[r, p * width + 2 * half : (p + 1) * width] = grad_v[:, here]
-            bias_sums[0:8, here] += fold(dqkv[r, p * width : p * width + half].astype(WIDE))
-        bias_sums[8:16, 0:C] += fold(grad_v.astype(WIDE))
 
     loop(T // 128, round_kv)
 
@@ -987,7 +981,17 @@
         red_step(0, s)
 
     loop(nt, first_back)
+    loop(blocks, grad_mix)
     loop(blocks, grad_qkv)
+
+    def sum_biases(i):
+        r = pl.ds(pl.multiple_of(i * 128, 128), 128)
+        for p in range(2):
+            here = slice(p * half, (p + 1) * half)
+            bias_sums[0:8, here] += fold(dqkv[r, p * width : p * width + half].astype(WIDE))
+            bias_sums[8:16, here] += fold(dqkv[r, p * width + 2 * half : (p + 1) * width].astype(WIDE))
+
+    loop(T // 128, sum_biases)
     due("heads")
 
     for j in range(4):

time: 169 us -> 169 us (level)
  no operation moved by 1% of the time
where the time goes in v2:
time: 169 us
  Pallas kernels  168 us (99%)
    pallas_call x1, Pallas kernels, layer(): pl.pallas_call(functools.partial(kernel, nd, nt), out_shape=[sds((T, D),...  161 us
    pallas_call x1, Pallas kernels, shards(): pl.pallas_call(update_kernel, out_shape=[sds(x.shape, x.dtype) for x in r...  7.14 us

profile of v2, /device:TPU:0, one launch (start us, length us, event | category | flops | bytes accessed | tf_op | source)
XLA Modules:
  0.0 169.0 jit_solution(10788090781530991779)
XLA Ops:
  0.6 161.0 %shard_map.351 = (bf16[1024,1024]{1,0:T(8,128)(2,1)}, bf16[1024,1024]{1,0:T(8,128)(2,1)}, f32[1,128,384]{2,1,0:T(8,128)}, f32[1,128,384]{2,1,0:T(8,128)}, f32[1,...) custom-call(bf16[1024,1024]{1,0:T(8,128)(2,1)} %tokens.1, ...), custom_call_target="tpu_custom_call" | custom-call | tf_op jit(solution)/shard_map/pallas_call | solution.py:1146
  161.7 7.1 %shard_map.352 = (bf16[1024,1024]{1,0:T(8,128)(2,1)}, bf16[1024,1024]{1,0:T(8,128)(2,1)}, f32[3,128,256]{2,1,0:T(8,128)}, f32[2,32]{1,0:T(2,128)}, f32[256,128]{...) custom-call(bf16[1024,1024]{1,0:T(8,128)(2,1)} %get-tuple-element.40, ...), custom_call_target="tpu_custom_call" | custom-call | tf_op jit(solution)/shard_map/pallas_call | solution.py:1257
